TPU v7x, 128 devices: a whole 4x4x4 slice. The times are simulated.
128 devices in a mesh: src: 8 (over x, z_hi), tgt: 16 (over y, z_lo, core).
Axes of the slice: x: 4, y: 4, z: 4 (z_hi: 2, z_lo: 2; z = z_hi * 2 + z_lo), core: 2. Of those that a mesh axis runs over, the one named last changes fastest.
Arguments:
- noise: bfloat16 [4096, 2048], P(('src', 'tgt')), may hold values from -6 to 6
- data: bfloat16 [4096, 2048], P(('src', 'tgt')), may hold values from -6 to 6
- t_index: int32 [4096], P(('src', 'tgt')), may hold values from 0 to 1000
- embed_weight: bfloat16 [64, 2048], replicated, may hold values from -0.75 to 0.75
- position: bfloat16 [32, 2048], replicated, may hold values from -6 to 6
- norm_gain: float32 [2048], replicated, may hold values from 0.5 to 1.5
- qkv_weight: bfloat16 [2048, 6144], P(None, 'tgt'), may hold values from -0.125 to 0.125
Outputs:
- velocity: bfloat16 [4096, 2048], P(('src', 'tgt'))
- qkv: bfloat16 [131072, 6144], P(('src', 'tgt'))
All inputs are finite; a program needn't handle non-finite values.
Results may differ from a plain program's by a relative error of at most 0.014.
Values may be sent and summed in bfloat16 or wider, within the bound.
No kernel may reach another device: no remote copies, remote signals or barrier semaphores. Data moves between devices by JAX's collectives and lax.ppermute only.
A program may use at most 448 MiB of HBM per device.

v0:
```python
import jax
import jax.numpy as jnp
from jax import lax
from jax.sharding import PartitionSpec as P

ITERS = 3
TGRID = 1000


def joined(value, axis, join):
    pieces = jax.tree.map(lambda part: lax.all_gather(part, axis), value)
    head = jax.tree.map(lambda part: part[0], pieces)
    tail = jax.tree.map(lambda part: part[1:], pieces)
    total, _ = lax.scan(lambda total, share: (join(total, share), None), head, tail)
    return total


def combine_lse(first, second):
    highest = jnp.maximum(first[0], second[0])
    return (
        highest,
        first[1] * jnp.exp(first[0] - highest) + second[1] * jnp.exp(second[0] - highest),
    )


def row_potential(scores, epsilon):
    local_peak = jnp.max(scores, axis=1)
    local_total = jnp.sum(jnp.exp(scores - local_peak[:, None]), axis=1)
    peak_all, total_all = joined((local_peak, local_total), "tgt", combine_lse)
    return -epsilon * (peak_all + jnp.log(total_all))


def col_potential(scores, epsilon):
    local_peak = jnp.max(scores, axis=0)
    local_total = jnp.sum(jnp.exp(scores - local_peak[None, :]), axis=0)
    peak_all, total_all = joined((local_peak, local_total), "src", combine_lse)
    return -epsilon * (peak_all + jnp.log(total_all))


def embed_rows(samples, embed_weight, position, norm_gain):
    count = samples.shape[0]
    patch_count = position.shape[0]
    patch_in = embed_weight.shape[0]
    width = embed_weight.shape[1]
    patches = samples.reshape(count * patch_count, patch_in)
    embedded = jnp.dot(patches, embed_weight, preferred_element_type=jnp.float32).reshape(
        count, patch_count, width
    )
    embedded = embedded + position.astype(jnp.float32)[None]
    meansq = jnp.mean(embedded * embedded, axis=-1, keepdims=True)
    normed = (embedded * lax.rsqrt(meansq + 1e-06) * norm_gain).astype(jnp.bfloat16)
    return normed.reshape(count * patch_count, width)


def local(noise, data, t_index, embed_weight, position, norm_gain, qkv_weight):
    latent = noise.shape[1]
    own_rows = noise.shape[0]
    noise_block = lax.all_gather(noise, "tgt", axis=0, tiled=True)
    data_block = lax.all_gather(data, "src", axis=0, tiled=True)
    noise_sq = jnp.sum(jnp.square(noise_block.astype(jnp.float32)), axis=1)
    data_sq = jnp.sum(jnp.square(data_block.astype(jnp.float32)), axis=1)
    cross_term = lax.dot_general(
        noise_block, data_block, (((1,), (1,)), ((), ())), preferred_element_type=jnp.float32
    )
    cost = (noise_sq[:, None] + data_sq[None, :] - 2.0 * cross_term) / latent
    col_pot = jnp.zeros((data_block.shape[0],), jnp.float32)
    row_pot = jnp.zeros((noise_block.shape[0],), jnp.float32)
    epsilon = 0.04
    for step in range(ITERS):
        epsilon = 0.04 * 0.45**step
        row_pot = row_potential((col_pot[None, :] - cost) / epsilon, epsilon)
        col_pot = col_potential((row_pot[:, None] - cost) / epsilon, epsilon)
    scores = (col_pot[None, :] - cost) / epsilon
    offset = lax.axis_index("tgt") * own_rows
    local_peak = jnp.max(scores, axis=1)
    local_total = jnp.sum(jnp.exp(scores - local_peak[:, None]), axis=1)
    peak_all, denom = joined((local_peak, local_total), "tgt", combine_lse)
    coupling = jnp.exp(scores - peak_all[:, None]).astype(jnp.bfloat16)
    partial_sum = jnp.dot(coupling, data_block, preferred_element_type=jnp.float32)
    numer = lax.psum_scatter(
        partial_sum.astype(jnp.bfloat16), "tgt", scatter_dimension=0, tiled=True
    ).astype(jnp.float32)
    own_denom = lax.dynamic_slice_in_dim(denom, offset, own_rows, 0)
    target = numer / own_denom[:, None]
    noise_own = noise.astype(jnp.float32)
    velocity = (target - noise_own).astype(jnp.bfloat16)
    times = t_index.astype(jnp.float32) / TGRID
    mixed = ((1.0 - times)[:, None] * noise_own + times[:, None] * target).astype(jnp.bfloat16)
    normed = embed_rows(mixed, embed_weight, position, norm_gain)
    qkv = jnp.dot(
        normed,
        lax.all_gather(qkv_weight, "tgt", axis=1, tiled=True),
        preferred_element_type=jnp.float32,
    ).astype(jnp.bfloat16)
    return (velocity, qkv)


def solution(mesh):
    return jax.shard_map(
        local,
        mesh=mesh,
        in_specs=(
            P(("src", "tgt"), None),
            P(("src", "tgt"), None),
            P(("src", "tgt")),
            P(),
            P(),
            P(),
            P(None, "tgt"),
        ),
        out_specs=(P(("src", "tgt"), None), P(("src", "tgt"), None)),
        check_vma=False,
    )
```

profile of v0, /device:TPU:1, one launch (start us, length us, event | category | flops | bytes accessed | tf_op | source)
XLA Modules:
  0.0 597.8 jit_solution(4102030687520857336)
XLA Ops:
  8.7 51.4 %all-gather.34.cloned.1.call-done = bf16[256,2048]{1,0:T(8,128)(2,1)} async-done(((bf16[32,2048]{1,0:T(8,128)(2,1)}), bf16[256,2048]{1,0:T(8,128)(2,1)}) %all-gather.34.cloned.1.call-update) | async-done | bytes 1048592 | tf_op jit(solution)/shard_map/all_gather | solution.py:59
  61.6 34.1 %all-gather.32.cloned.1.call-done = bf16[512,2048]{1,0:T(8,128)(2,1)} async-done(((bf16[32,2048]{1,0:T(8,128)(2,1)}), bf16[512,2048]{1,0:T(8,128)(2,1)}) %all-gather.32.cloned.1.call-update) | async-done | bytes 2097168 | tf_op jit(solution)/shard_map/all_gather | solution.py:58
  95.7 2.1 multiply_reduce_fusion.1
  97.7 2.7 fusion.2
  100.6 18.1 %all-gather.15 = f32[16,1,512]{2,1,0:T(1,128)S(1)} all-gather(f32[1,1,512]{2,1,0:T(1,128)S(1)} %bitcast.176), channel_id=3, replica_groups=mesh['src'=8,'tgt'=16] {'tgt'}, dimensions={0}, use_global_device_ids=true | all-gather | bytes 34816 | tf_op jit(solution)/shard_map/all_gather | solution.py:11
  118.8 16.3 %all-gather.14 = f32[16,1,512]{2,1,0:T(1,128)S(1)} all-gather(f32[1,1,512]{2,1,0:T(1,128)S(1)} %bitcast.173), channel_id=2, replica_groups=mesh['src'=8,'tgt'=16] {'tgt'}, dimensions={0}, use_global_device_ids=true | all-gather | bytes 34816 | tf_op jit(solution)/shard_map/all_gather | solution.py:11
  136.3 19.5 %all-gather.16 = f32[8,1,256]{2,1,0:T(1,128)S(1)} all-gather(f32[1,1,256]{2,1,0:T(1,128)S(1)} %bitcast.170), channel_id=4, replica_groups=mesh['src'=8,'tgt'=16] {'src'}, dimensions={0}, use_global_device_ids=true | all-gather | bytes 9216 | tf_op jit(solution)/shard_map/all_gather | solution.py:11
  155.8 14.6 %all-gather.17 = f32[8,1,256]{2,1,0:T(1,128)S(1)} all-gather(f32[1,1,256]{2,1,0:T(1,128)S(1)} %bitcast.178), channel_id=5, replica_groups=mesh['src'=8,'tgt'=16] {'src'}, dimensions={0}, use_global_device_ids=true | all-gather | bytes 9216 | tf_op jit(solution)/shard_map/all_gather | solution.py:11
  171.1 24.3 %all-gather.19 = f32[16,1,512]{2,1,0:T(1,128)S(1)} all-gather(f32[1,1,512]{2,1,0:T(1,128)S(1)} %bitcast.174), channel_id=7, replica_groups=mesh['src'=8,'tgt'=16] {'tgt'}, dimensions={0}, use_global_device_ids=true | all-gather | bytes 34816 | tf_op jit(solution)/shard_map/all_gather | solution.py:11
  195.5 16.9 %all-gather.18 = f32[16,1,512]{2,1,0:T(1,128)S(1)} all-gather(f32[1,1,512]{2,1,0:T(1,128)S(1)} %bitcast.167), channel_id=6, replica_groups=mesh['src'=8,'tgt'=16] {'tgt'}, dimensions={0}, use_global_device_ids=true | all-gather | bytes 34816 | tf_op jit(solution)/shard_map/all_gather | solution.py:11
  213.6 17.9 %all-gather.20 = f32[8,1,256]{2,1,0:T(1,128)S(1)} all-gather(f32[1,1,256]{2,1,0:T(1,128)S(1)} %bitcast.171), channel_id=8, replica_groups=mesh['src'=8,'tgt'=16] {'src'}, dimensions={0}, use_global_device_ids=true | all-gather | bytes 9216 | tf_op jit(solution)/shard_map/all_gather | solution.py:11
  231.4 14.6 %all-gather.21 = f32[8,1,256]{2,1,0:T(1,128)S(1)} all-gather(f32[1,1,256]{2,1,0:T(1,128)S(1)} %bitcast.179), channel_id=9, replica_groups=mesh['src'=8,'tgt'=16] {'src'}, dimensions={0}, use_global_device_ids=true | all-gather | bytes 9216 | tf_op jit(solution)/shard_map/all_gather | solution.py:11
  246.8 24.3 %all-gather.23 = f32[16,1,512]{2,1,0:T(1,128)S(1)} all-gather(f32[1,1,512]{2,1,0:T(1,128)S(1)} %bitcast.175), channel_id=11, replica_groups=mesh['src'=8,'tgt'=16] {'tgt'}, dimensions={0}, use_global_device_ids=true | all-gather | bytes 34816 | tf_op jit(solution)/shard_map/all_gather | solution.py:11
  271.1 16.9 %all-gather.22 = f32[16,1,512]{2,1,0:T(1,128)S(1)} all-gather(f32[1,1,512]{2,1,0:T(1,128)S(1)} %bitcast.168), channel_id=10, replica_groups=mesh['src'=8,'tgt'=16] {'tgt'}, dimensions={0}, use_global_device_ids=true | all-gather | bytes 34816 | tf_op jit(solution)/shard_map/all_gather | solution.py:11
  289.2 17.9 %all-gather.24 = f32[8,1,256]{2,1,0:T(1,128)S(1)} all-gather(f32[1,1,256]{2,1,0:T(1,128)S(1)} %bitcast.172), channel_id=12, replica_groups=mesh['src'=8,'tgt'=16] {'src'}, dimensions={0}, use_global_device_ids=true | all-gather | bytes 9216 | tf_op jit(solution)/shard_map/all_gather | solution.py:11
  307.1 14.6 %all-gather.25 = f32[8,1,256]{2,1,0:T(1,128)S(1)} all-gather(f32[1,1,256]{2,1,0:T(1,128)S(1)} %bitcast.180), channel_id=13, replica_groups=mesh['src'=8,'tgt'=16] {'src'}, dimensions={0}, use_global_device_ids=true | all-gather | bytes 9216 | tf_op jit(solution)/shard_map/all_gather | solution.py:11
  322.4 24.3 %all-gather.27 = f32[16,1,512]{2,1,0:T(1,128)S(1)} all-gather(f32[1,1,512]{2,1,0:T(1,128)S(1)} %bitcast.177), channel_id=15, replica_groups=mesh['src'=8,'tgt'=16] {'tgt'}, dimensions={0}, use_global_device_ids=true | all-gather | bytes 34816 | tf_op jit(solution)/shard_map/all_gather | solution.py:11
  346.7 16.9 %all-gather.26 = f32[16,1,512]{2,1,0:T(1,128)S(1)} all-gather(f32[1,1,512]{2,1,0:T(1,128)S(1)} %bitcast.169), channel_id=14, replica_groups=mesh['src'=8,'tgt'=16] {'tgt'}, dimensions={0}, use_global_device_ids=true | all-gather | bytes 34816 | tf_op jit(solution)/shard_map/all_gather | solution.py:11
  364.5 2.2 convolution_convert_fusion.1
  367.5 56.1 %reduce-scatter.2.cloned.1.call-done = bf16[32,2048]{1,0:T(8,128)(2,1)} async-done(((bf16[512,2048]{1,0:T(8,128)(2,1)}), bf16[32,2048]{1,0:T(8,128)(2,1)}) %reduce-scatter.2.cloned.1.call-update) | async-done | bytes 131088 | tf_op jit(solution)/shard_map/reduce_scatter | solution.py:80
  423.6 1.7 fusion.11
  426.9 3.0 multiply_convert_fusion
  430.0 129.0 %all-gather.36.cloned.1.call-done = bf16[2048,6144]{1,0:T(8,128)(2,1)} async-done(((bf16[2048,384]{1,0:T(8,128)(2,1)}), bf16[2048,6144]{1,0:T(8,128)(2,1)}) %all-gather.36.cloned.1.call-update) | async-done | bytes 25165840 | tf_op jit(solution)/shard_map/all_gather | solution.py:92
  558.9 32.3 %convolution_convert_fusion = bf16[1024,6144]{1,0:T(8,128)(2,1)} fusion(bf16[1024,2048]{1,0:T(8,128)(2,1)} %bitcast.124, bf16[2048,6144]{1,0:T(8,128)(2,1)} %all-gather.36.cloned.1.call-done), kind=kOutput, calls=%fused_computation.21 | convolution fusion | flops 25776095232 | bytes 41943040 | tf_op jit(solution)/shard_map/dot_general | solution.py:90
  (257 shorter events, 14.4 us)
Async XLA Ops:
  7.2 418.4 %copy-start = (bf16[64,2048]{1,0:T(8,128)(2,1)S(1)}, bf16[64,2048]{1,0:T(8,128)(2,1)}, u32[]{:S(2)}) copy-start(bf16[64,2048]{1,0:T(8,128)(2,1)} %param.24) | copy-start | bytes 786436
  7.2 52.9 %all-gather.34.cloned.1.call-start = ((), (), s32[]{:S(2)}) async-start(), calls=%async_computation.2 | async-start | bytes 1179648 | tf_op jit(solution)/shard_map/all_gather | solution.py:59
  7.9 87.7 %all-gather.32.cloned.1.call-start = ((), (), s32[]{:S(2)}) async-start(), calls=%async_computation.1 | async-start | bytes 2228224 | tf_op jit(solution)/shard_map/all_gather | solution.py:58
  8.7 414.9 %reduce-scatter.2.cloned.1.call-start = ((), (), s32[]{:S(2)}) async-start(), calls=%async_computation.3 | async-start | bytes 2228224 | tf_op jit(solution)/shard_map/reduce_scatter | solution.py:80
  97.7 266.8 %copy-start.1 = (bf16[256,2048]{1,0:T(8,128)(2,1)S(1)}, bf16[256,2048]{1,0:T(8,128)(2,1)}, u32[]{:S(2)}) copy-start(bf16[256,2048]{1,0:T(8,128)(2,1)} %all-gather.34.cloned.1.call-done) | copy-start | bytes 3145732
  135.9 231.4 %copy-start.3 = (bf16[32,2048]{1,0:T(8,128)(2,1)S(1)}, bf16[32,2048]{1,0:T(8,128)(2,1)}, u32[]{:S(2)}) copy-start(bf16[32,2048]{1,0:T(8,128)(2,1)} %param.25) | copy-start | bytes 393220
  135.9 231.4 %copy-start.5 = (s32[32]{0:T(128)S(1)}, s32[32]{0:T(128)}, u32[]{:S(2)}) copy-start(s32[32]{0:T(128)} %param.23) | copy-start | bytes 388
  135.9 287.7 %copy-start.2 = (bf16[32,2048]{1,0:T(8,128)(2,1)S(1)}, bf16[32,2048]{1,0:T(8,128)(2,1)}, u32[]{:S(2)}) copy-start(bf16[32,2048]{1,0:T(8,128)(2,1)} %param.21) | copy-start | bytes 393220
  364.5 62.4 %copy-start.4 = (f32[2048]{0:T(1024)S(1)}, f32[2048]{0:T(1024)}, u32[]{:S(2)}) copy-start(f32[2048]{0:T(1024)} %param.26) | copy-start | bytes 24580
  366.7 192.2 %all-gather.36.cloned.1.call-start = ((), (), s32[]{:S(2)}) async-start(), calls=%async_computation.4 | async-start | bytes 26738688 | tf_op jit(solution)/shard_map/all_gather | solution.py:92
Sparse Core Ops, SparseCore 0:
  10.4 49.6 all-gather.33
  61.8 33.8 all-gather.31
  366.9 56.7 reduce-scatter.1
  425.1 133.7 all-gather.35
where the time goes:
time: 598 us
  waiting for transfers between devices  272 us (45%)
  blocking collectives  257 us (43%)
  matrix products  38.6 us (6%)
  between operations  14.1 us (2%)
  other arithmetic  12.3 us (2%)
    all_gather x14, blocking collectives, joined(): pieces = jax.tree.map(lambda part: lax.all_gather(part, axis), value)  257 us
    all_gather x1, waiting for transfers between devices, local(): lax.all_gather(qkv_weight, 'tgt', axis=1, tiled=True)  129 us
    reduce_scatter x1, waiting for transfers between devices, local(): lax.psum_scatter(partial_sum.astype(jnp.bfloat16), 'tgt', scatter_dimensi...  56.1 us
    all_gather x1, waiting for transfers between devices, local(): data_block = lax.all_gather(data, 'src', axis=0, tiled=True)  51.4 us
    all_gather x1, waiting for transfers between devices, local(): noise_block = lax.all_gather(noise, 'tgt', axis=0, tiled=True)  34.1 us
    dot_general x1, matrix products, local(): jnp.dot(normed, lax.all_gather(qkv_weight, 'tgt', axis=1, tiled=True), pr...  32.3 us
  transfers between devices with their start and end apart: 4, of which 4 were waited for; matrix products, arithmetic and copies ran while one was open for 1% of the time, Pallas kernels for 0%

commit v1 on v0

--- a/solution.py
+++ b/solution.py
@@ -56,7 +56,8 @@
     latent = noise.shape[1]
     own_rows = noise.shape[0]
     noise_block = lax.all_gather(noise, "tgt", axis=0, tiled=True)
-    data_block = lax.all_gather(data, "src", axis=0, tiled=True)
+    stack = jnp.stack([data] * lax.axis_size("src"))
+    data_block = jnp.concatenate(lax.all_to_all(stack, "src", 0, 0), axis=0)
     noise_sq = jnp.sum(jnp.square(noise_block.astype(jnp.float32)), axis=1)
     data_sq = jnp.sum(jnp.square(data_block.astype(jnp.float32)), axis=1)
     cross_term = lax.dot_general(

time: 598 us -> 557 us (0.931)
  waiting for transfers between devices: 272 us -> 221 us
  starting transfers between devices: 0.34 us -> 8.46 us
    all_gather x1 -> x0, waiting for transfers between devices: 51.4 us -> none  [local(): data_block = lax.all_gather(data, 'src', axis=0, tiled=True)]
    all_to_all x0 -> x1, waiting for transfers between devices: none -> 15.5 us  [local(): data_block = jnp.concatenate(lax.all_to_all(stack, 'src', 0, 0), axis=0)]
    all_gather x1, waiting for transfers between devices: 34.1 us -> 18.9 us  [local(): noise_block = lax.all_gather(noise, 'tgt', axis=0, tiled=True)]
    all_to_all x0 -> x1, starting transfers between devices: none -> 8.16 us  [local(): data_block = jnp.concatenate(lax.all_to_all(stack, 'src', 0, 0), axis=0)]
  transfers between devices with their start and end apart: 4 -> 4, of which waited for: 4 -> 4; matrix products, arithmetic and copies ran while one was open for 1% -> 2% of each run, Pallas kernels for 0% -> 0%
where the time goes in v1:
time: 557 us; the launch traced here: 556 us
  blocking collectives  259 us (46%)
  waiting for transfers between devices  221 us (40%)
  matrix products  38.2 us (7%)
  between operations  14 us (3%)
  other arithmetic  11 us (2%)
  starting transfers between devices  8.46 us (2%)
    all_gather x14, blocking collectives, joined(): pieces = jax.tree.map(lambda part: lax.all_gather(part, axis), value)  259 us
    all_gather x1, waiting for transfers between devices, local(): lax.all_gather(qkv_weight, 'tgt', axis=1, tiled=True)  129 us
    reduce_scatter x1, waiting for transfers between devices, local(): lax.psum_scatter(partial_sum.astype(jnp.bfloat16), 'tgt', scatter_dimensi...  56.1 us
    dot_general x1, matrix products, local(): jnp.dot(normed, lax.all_gather(qkv_weight, 'tgt', axis=1, tiled=True), pr...  32.3 us
    all_gather x1, waiting for transfers between devices, local(): noise_block = lax.all_gather(noise, 'tgt', axis=0, tiled=True)  18.9 us
    all_to_all x1, waiting for transfers between devices, local(): data_block = jnp.concatenate(lax.all_to_all(stack, 'src', 0, 0), axis=0)  15.5 us
  transfers between devices with their start and end apart: 4, of which 4 were waited for; matrix products, arithmetic and copies ran while one was open for 2% of the time, Pallas kernels for 0%

profile of v1, /device:TPU:1, one launch (start us, length us, event | category | flops | bytes accessed | tf_op | source)
XLA Modules:
  0.0 556.5 jit_solution(14260734142323233431)
XLA Ops:
  9.9 8.2 %all-to-all-start = ((bf16[8,32,2048]{2,1,0:T(8,128)(2,1)}), bf16[8,32,2048]{2,1,0:T(8,128)(2,1)S(1)}, u32[]{:S(2)}, u32[]{:S(2)}) async-start(bf16[8,32,2048]{2,1,0:T(8,128)(2,1)} %stack.2), calls=%async_computation | async-start | bytes 2097152 | tf_op jit(solution)/shard_map/all_to_all | solution.py:60
  18.1 15.5 %all-to-all-done = bf16[8,32,2048]{2,1,0:T(8,128)(2,1)S(1)} async-done(((bf16[8,32,2048]{2,1,0:T(8,128)(2,1)}), bf16[8,32,2048]{2,1,0:T(8,128)(2,1)S(1)}, u32[]{:S(2)}, u32[]{:S(2)}) %all-to-all-start) | async-done | bytes 1048608 | tf_op jit(solution)/shard_map/all_to_all | solution.py:60
  34.0 18.9 %all-gather.31.cloned.1.call-done = bf16[512,2048]{1,0:T(8,128)(2,1)} async-done(((bf16[32,2048]{1,0:T(8,128)(2,1)}), bf16[512,2048]{1,0:T(8,128)(2,1)}) %all-gather.31.cloned.1.call-update) | async-done | bytes 2097168 | tf_op jit(solution)/shard_map/all_gather | solution.py:58
  52.8 2.1 multiply_reduce_fusion.1
  54.9 2.4 fusion.2
  57.4 18.1 %all-gather.15 = f32[16,1,512]{2,1,0:T(1,128)S(1)} all-gather(f32[1,1,512]{2,1,0:T(1,128)S(1)} %bitcast.179), channel_id=3, replica_groups=mesh['src'=8,'tgt'=16] {'tgt'}, dimensions={0}, use_global_device_ids=true | all-gather | bytes 34816 | tf_op jit(solution)/shard_map/all_gather | solution.py:11
  75.6 16.3 %all-gather.14 = f32[16,1,512]{2,1,0:T(1,128)S(1)} all-gather(f32[1,1,512]{2,1,0:T(1,128)S(1)} %bitcast.176), channel_id=2, replica_groups=mesh['src'=8,'tgt'=16] {'tgt'}, dimensions={0}, use_global_device_ids=true | all-gather | bytes 34816 | tf_op jit(solution)/shard_map/all_gather | solution.py:11
  93.1 21.4 %all-gather.16 = f32[8,1,256]{2,1,0:T(1,128)S(1)} all-gather(f32[1,1,256]{2,1,0:T(1,128)S(1)} %bitcast.173), channel_id=4, replica_groups=mesh['src'=8,'tgt'=16] {'src'}, dimensions={0}, use_global_device_ids=true | all-gather | bytes 9216 | tf_op jit(solution)/shard_map/all_gather | solution.py:11
  114.5 14.6 %all-gather.17 = f32[8,1,256]{2,1,0:T(1,128)S(1)} all-gather(f32[1,1,256]{2,1,0:T(1,128)S(1)} %bitcast.181), channel_id=5, replica_groups=mesh['src'=8,'tgt'=16] {'src'}, dimensions={0}, use_global_device_ids=true | all-gather | bytes 9216 | tf_op jit(solution)/shard_map/all_gather | solution.py:11
  129.8 24.3 %all-gather.19 = f32[16,1,512]{2,1,0:T(1,128)S(1)} all-gather(f32[1,1,512]{2,1,0:T(1,128)S(1)} %bitcast.177), channel_id=7, replica_groups=mesh['src'=8,'tgt'=16] {'tgt'}, dimensions={0}, use_global_device_ids=true | all-gather | bytes 34816 | tf_op jit(solution)/shard_map/all_gather | solution.py:11
  154.1 16.9 %all-gather.18 = f32[16,1,512]{2,1,0:T(1,128)S(1)} all-gather(f32[1,1,512]{2,1,0:T(1,128)S(1)} %bitcast.170), channel_id=6, replica_groups=mesh['src'=8,'tgt'=16] {'tgt'}, dimensions={0}, use_global_device_ids=true | all-gather | bytes 34816 | tf_op jit(solution)/shard_map/all_gather | solution.py:11
  172.3 17.9 %all-gather.20 = f32[8,1,256]{2,1,0:T(1,128)S(1)} all-gather(f32[1,1,256]{2,1,0:T(1,128)S(1)} %bitcast.174), channel_id=8, replica_groups=mesh['src'=8,'tgt'=16] {'src'}, dimensions={0}, use_global_device_ids=true | all-gather | bytes 9216 | tf_op jit(solution)/shard_map/all_gather | solution.py:11
  190.1 14.6 %all-gather.21 = f32[8,1,256]{2,1,0:T(1,128)S(1)} all-gather(f32[1,1,256]{2,1,0:T(1,128)S(1)} %bitcast.182), channel_id=9, replica_groups=mesh['src'=8,'tgt'=16] {'src'}, dimensions={0}, use_global_device_ids=true | all-gather | bytes 9216 | tf_op jit(solution)/shard_map/all_gather | solution.py:11
  205.5 24.3 %all-gather.23 = f32[16,1,512]{2,1,0:T(1,128)S(1)} all-gather(f32[1,1,512]{2,1,0:T(1,128)S(1)} %bitcast.178), channel_id=11, replica_groups=mesh['src'=8,'tgt'=16] {'tgt'}, dimensions={0}, use_global_device_ids=true | all-gather | bytes 34816 | tf_op jit(solution)/shard_map/all_gather | solution.py:11
  229.8 16.9 %all-gather.22 = f32[16,1,512]{2,1,0:T(1,128)S(1)} all-gather(f32[1,1,512]{2,1,0:T(1,128)S(1)} %bitcast.171), channel_id=10, replica_groups=mesh['src'=8,'tgt'=16] {'tgt'}, dimensions={0}, use_global_device_ids=true | all-gather | bytes 34816 | tf_op jit(solution)/shard_map/all_gather | solution.py:11
  247.9 17.9 %all-gather.24 = f32[8,1,256]{2,1,0:T(1,128)S(1)} all-gather(f32[1,1,256]{2,1,0:T(1,128)S(1)} %bitcast.175), channel_id=12, replica_groups=mesh['src'=8,'tgt'=16] {'src'}, dimensions={0}, use_global_device_ids=true | all-gather | bytes 9216 | tf_op jit(solution)/shard_map/all_gather | solution.py:11
  265.8 14.6 %all-gather.25 = f32[8,1,256]{2,1,0:T(1,128)S(1)} all-gather(f32[1,1,256]{2,1,0:T(1,128)S(1)} %bitcast.183), channel_id=13, replica_groups=mesh['src'=8,'tgt'=16] {'src'}, dimensions={0}, use_global_device_ids=true | all-gather | bytes 9216 | tf_op jit(solution)/shard_map/all_gather | solution.py:11
  281.1 24.3 %all-gather.27 = f32[16,1,512]{2,1,0:T(1,128)S(1)} all-gather(f32[1,1,512]{2,1,0:T(1,128)S(1)} %bitcast.180), channel_id=15, replica_groups=mesh['src'=8,'tgt'=16] {'tgt'}, dimensions={0}, use_global_device_ids=true | all-gather | bytes 34816 | tf_op jit(solution)/shard_map/all_gather | solution.py:11
  305.4 16.9 %all-gather.26 = f32[16,1,512]{2,1,0:T(1,128)S(1)} all-gather(f32[1,1,512]{2,1,0:T(1,128)S(1)} %bitcast.172), channel_id=14, replica_groups=mesh['src'=8,'tgt'=16] {'tgt'}, dimensions={0}, use_global_device_ids=true | all-gather | bytes 34816 | tf_op jit(solution)/shard_map/all_gather | solution.py:11
  323.2 2.2 convolution_convert_fusion.1
  326.3 56.1 %reduce-scatter.2.cloned.1.call-done = bf16[32,2048]{1,0:T(8,128)(2,1)} async-done(((bf16[512,2048]{1,0:T(8,128)(2,1)}), bf16[32,2048]{1,0:T(8,128)(2,1)}) %reduce-scatter.2.cloned.1.call-update) | async-done | bytes 131088 | tf_op jit(solution)/shard_map/reduce_scatter | solution.py:81
  385.7 3.0 multiply_convert_fusion
  388.7 128.9 %all-gather.33.cloned.1.call-done = bf16[2048,6144]{1,0:T(8,128)(2,1)} async-done(((bf16[2048,384]{1,0:T(8,128)(2,1)}), bf16[2048,6144]{1,0:T(8,128)(2,1)}) %all-gather.33.cloned.1.call-update) | async-done | bytes 25165840 | tf_op jit(solution)/shard_map/all_gather | solution.py:93
  517.6 32.3 %convolution_convert_fusion = bf16[1024,6144]{1,0:T(8,128)(2,1)} fusion(bf16[1024,2048]{1,0:T(8,128)(2,1)} %bitcast.127, bf16[2048,6144]{1,0:T(8,128)(2,1)} %all-gather.33.cloned.1.call-done), kind=kOutput, calls=%fused_computation.21 | convolution fusion | flops 25776095232 | bytes 41943040 | tf_op jit(solution)/shard_map/dot_general | solution.py:91
  (256 shorter events, 16.4 us)
Async XLA Ops:
  7.2 377.2 %copy-start = (bf16[64,2048]{1,0:T(8,128)(2,1)S(1)}, bf16[64,2048]{1,0:T(8,128)(2,1)}, u32[]{:S(2)}) copy-start(bf16[64,2048]{1,0:T(8,128)(2,1)} %param.24) | copy-start | bytes 786436
  7.2 45.7 %all-gather.31.cloned.1.call-start = ((), (), s32[]{:S(2)}) async-start(), calls=%async_computation.2 | async-start | bytes 2228224 | tf_op jit(solution)/shard_map/all_gather | solution.py:58
  9.9 23.7 %all-to-all-start = ((bf16[8,32,2048]{2,1,0:T(8,128)(2,1)}), bf16[8,32,2048]{2,1,0:T(8,128)(2,1)S(1)}, u32[]{:S(2)}, u32[]{:S(2)}) async-start(bf16[8,32,2048]{2,1,0:T(8,128)(2,1)} %stack.2), calls=%async_computation | async-start | bytes 2097152 | tf_op jit(solution)/shard_map/all_to_all | solution.py:60
  18.1 364.3 %reduce-scatter.2.cloned.1.call-start = ((), (), s32[]{:S(2)}) async-start(), calls=%async_computation.3 | async-start | bytes 2228224 | tf_op jit(solution)/shard_map/reduce_scatter | solution.py:81
  92.7 233.4 %copy-start.2 = (bf16[32,2048]{1,0:T(8,128)(2,1)S(1)}, bf16[32,2048]{1,0:T(8,128)(2,1)}, u32[]{:S(2)}) copy-start(bf16[32,2048]{1,0:T(8,128)(2,1)} %param.25) | copy-start | bytes 393220
  92.7 233.5 %copy-start.4 = (s32[32]{0:T(128)S(1)}, s32[32]{0:T(128)}, u32[]{:S(2)}) copy-start(s32[32]{0:T(128)} %param.23) | copy-start | bytes 388
  92.8 289.6 %copy-start.1 = (bf16[32,2048]{1,0:T(8,128)(2,1)S(1)}, bf16[32,2048]{1,0:T(8,128)(2,1)}, u32[]{:S(2)}) copy-start(bf16[32,2048]{1,0:T(8,128)(2,1)} %param.21) | copy-start | bytes 393220
  323.2 62.5 %copy-start.3 = (f32[2048]{0:T(1024)S(1)}, f32[2048]{0:T(1024)}, u32[]{:S(2)}) copy-start(f32[2048]{0:T(1024)} %param.26) | copy-start | bytes 24580
  325.4 192.2 %all-gather.33.cloned.1.call-start = ((), (), s32[]{:S(2)}) async-start(), calls=%async_computation.4 | async-start | bytes 26738688 | tf_op jit(solution)/shard_map/all_gather | solution.py:93
Sparse Core Ops, SparseCore 0:
  9.7 43.0 all-gather.30
  325.5 56.7 reduce-scatter.1
  384.1 133.5 all-gather.32
